TPU v7x, 32 devices: a whole 2x2x4 slice. The times are simulated.
32 devices in a mesh: groups: 2 (over y), dp: 16 (over z, x, core).
Axes of the slice: x: 2, y: 2, z: 4, core: 2. Of those that a mesh axis runs over, the one named last changes fastest.
Arguments:
- train_acts: bfloat16 [4096, 27648], P(('groups', 'dp')), parts along dimension 0, may hold values from -6 to 6
- train_grads: bfloat16 [4096, 5120], P(('groups', 'dp')), parts along dimension 0, may hold values from -6 to 6
- seq_lengths: int32 [32], P(('groups', 'dp')), parts along dimension 0, may hold values from 32 to 128, as said below
- basis_out: bfloat16 [5120, 256], P('dp'), may hold values from -0.078125 to 0.078125
- basis_in: bfloat16 [27648, 384], P('dp'), may hold values from -0.0390625 to 0.0390625
- eigenvalues: float32 [256, 384], replicated, may hold values from 0.5 to 8
- query_grads: bfloat16 [5120, 1024], P('dp', 'groups'), parts along dimension 1, may hold values from -0.059814453 to 0.059814453
- query_acts: bfloat16 [27648, 1024], P('dp', 'groups'), parts along dimension 1, may hold values from -0.119628906 to 0.119628906
- candidates: int32 [32, 8], P(('groups', 'dp')), parts along dimension 0, may hold values from 0 to 31, all different within a row
Outputs:
- scores: float32 [32, 8], P(('groups', 'dp')), parts along dimension 0
There are 2 independent parts, one for each index of `groups`. A program takes and returns all parts, laid end to end along the dimension named above; an argument that names none is the same for every part. Nothing has to cross between parts.
Inputs may be any that keep to these rules, and one draw needn't show every extreme that they name: Sequence s fills slots 0 to seq_lengths[s] - 1 of its 128 slots; the rest are padding. `candidates`: each row names 8 different queries.
All inputs are finite; a program needn't handle non-finite values.
Results may differ from a plain program's by a relative error of at most 0.013.
Values may be sent and summed in bfloat16 or wider, within the bound.
A program may use at most 128 MiB of HBM per device.

v0:
```python
import jax
import jax.numpy as jnp
from jax import lax
from jax.sharding import PartitionSpec as P

NQ = 32
QLEN = 16


def shards(
    train_acts,
    train_grads,
    seq_lengths,
    basis_out,
    basis_in,
    eigenvalues,
    query_grads,
    query_acts,
    candidates,
):
    tok_dev = train_acts.shape[0]
    rank_out = basis_out.shape[1]
    rank_in = basis_in.shape[1]
    columns = train_grads
    g_full = jnp.dot(
        columns,
        lax.all_gather(basis_out, "dp", axis=0, tiled=True),
        preferred_element_type=jnp.float32,
    )
    living = (jnp.arange(tok_dev, dtype=jnp.int32) < seq_lengths[0])[:, None]
    g_rot = jnp.where(living, g_full, jnp.zeros_like(g_full)).astype(jnp.bfloat16)
    contract = (((0,), (0,)), ((), ()))
    out_part = lax.dot_general(query_grads, basis_out, contract, preferred_element_type=jnp.float32)
    in_part = lax.dot_general(query_acts, basis_in, contract, preferred_element_type=jnp.float32)
    out_total, in_total = lax.psum((out_part, in_part), "dp")
    q_out = out_total.astype(jnp.bfloat16)
    q_in = in_total.astype(jnp.bfloat16)
    joint = jnp.einsum(
        "qui,quj->qij",
        q_out.reshape(NQ, QLEN, rank_out),
        q_in.reshape(NQ, QLEN, rank_in),
        preferred_element_type=jnp.float32,
    )
    damping = 0.1 * jnp.mean(eigenvalues)
    precond = (joint / (eigenvalues + damping)).astype(jnp.bfloat16).reshape(NQ, rank_out * rank_in)
    precond = lax.optimization_barrier(precond)
    flat_contract = (((1,), (1,)), ((), ()))
    columns = train_acts
    a_full = jnp.dot(
        columns,
        lax.all_gather(basis_in, "dp", axis=0, tiled=True),
        preferred_element_type=jnp.float32,
    )
    a_rot = a_full.astype(jnp.bfloat16)
    train_rot = lax.dot_general(g_rot, a_rot, contract, preferred_element_type=jnp.float32).astype(
        jnp.bfloat16
    )
    totals = lax.dot_general(
        train_rot.reshape(1, rank_out * rank_in),
        precond,
        flat_contract,
        preferred_element_type=jnp.float32,
    )
    matches = candidates[:, :, None] == jnp.arange(NQ, dtype=jnp.int32)[None, None, :]
    return jnp.sum(jnp.where(matches, totals[:, None, :], jnp.zeros((), jnp.float32)), axis=2)


def solution(mesh):
    placed = (
        P(("groups", "dp"), None),
        P(("groups", "dp"), None),
        P(("groups", "dp")),
        P("dp", None),
        P("dp", None),
        P(),
        P("dp", "groups"),
        P("dp", "groups"),
        P(("groups", "dp"), None),
    )
    return jax.shard_map(
        shards, mesh=mesh, in_specs=placed, out_specs=P(("groups", "dp"), None), check_vma=False
    )
```

profile of v0, /device:TPU:9, one launch (start us, length us, event | category | flops | bytes accessed | tf_op | source)
XLA Modules:
  0.0 207.2 jit_solution(5239685337117426091)
XLA Ops:
  6.5 0.0 copy-start
  6.5 0.0 copy-start.1
  6.5 0.0 all-gather.5.cloned.1.call-start
  6.5 0.7 all-gather.5.cloned.1.call-update
  7.3 0.0 copy-start.2
  7.3 0.0 all-gather.3.cloned.1.call-start
  7.3 0.7 all-gather.3.cloned.1.call-update
  8.7 2.2 %fusion.5 = f32[512,256]{1,0:T(8,128)} fusion(bf16[320,512]{1,0:T(8,128)(2,1)} %param.15, bf16[320,256]{1,0:T(8,128)(2,1)} %param.12), kind=kOutput, calls=%fused_computation.14 | convolution fusion | flops 83886080 | bytes 1015808 | tf_op jit(solution)/shard_map/dot_general | solution.py:33
  10.8 0.0 copy-done
  10.8 0.0 copy-done.1
  10.8 2.0 fusion.6
  12.9 0.0 copy-done.2
  12.9 0.7 reduce_sum.20
  14.3 79.1 %all-reduce.2 = (bf16[512,256]{1,0:T(8,128)(2,1)S(1)}, bf16[512,384]{1,0:T(8,128)(2,1)S(1)}) all-reduce(f32[512,256]{1,0:T(8,128)} %fusion.5, f32[512,384]{1,0:T(8,128)} %fusion.6), channel_id=1, replica_groups=mesh['groups'=2,'dp'=16] {'dp'}, use_global_device_ids=true, to_apply=%region_0.1 | all-reduce | flops 327680 | bytes 1966080 | tf_op jit(solution)/shard_map/psum | solution.py:35
  93.3 1.8 divide_convert_fusion
  95.2 6.5 %copy.11 = bf16[4,8,256,384]{3,1,2,0:T(8,128)(2,1)} copy(bf16[4,8,256,384]{3,2,1,0:T(8,128)(2,1)S(1)} %bitcast.29) | data formatting | bytes 12582912
  101.7 0.0 copy-start.3
  101.7 36.0 %all-gather.5.cloned.1.call-done = bf16[27648,384]{1,0:T(8,128)(2,1)} async-done(((bf16[1728,384]{1,0:T(8,128)(2,1)}), bf16[27648,384]{1,0:T(8,128)(2,1)}) %all-gather.5.cloned.1.call-update) | async-done | bytes 21233680 | tf_op jit(solution)/shard_map/all_gather | solution.py:51
  137.7 12.9 %convolution_convert_fusion.1 = bf16[128,384]{1,0:T(8,128)(2,1)S(1)} fusion(bf16[128,27648]{1,0:T(8,128)(2,1)} %param.9, bf16[27648,384]{1,0:T(8,128)(2,1)} %all-gather.5.cloned.1.call-done), kind=kOutput, calls=%fused_computation.3 | convolution fusion | flops 2717958144 | bytes 28409856 | tf_op jit(solution)/shard_map/dot_general | solution.py:49
  150.7 41.6 %all-gather.3.cloned.1.call-done = bf16[5120,256]{1,0:T(8,128)(2,1)} async-done(((bf16[320,256]{1,0:T(8,128)(2,1)}), bf16[5120,256]{1,0:T(8,128)(2,1)}) %all-gather.3.cloned.1.call-update) | async-done | bytes 2621456 | tf_op jit(solution)/shard_map/all_gather | solution.py:27
  192.3 0.0 copy-done.3
  192.3 2.6 %fusion = bf16[1,1,256,384]{3,2,1,0:T(8,128)(2,1)S(1)} fusion(bf16[128,384]{1,0:T(8,128)(2,1)S(1)} %convolution_convert_fusion.1, bf16[128,5120]{1,0:T(8,128)(2,1)S(1)} %copy-done.3, bf16[5120,256]{1,0:T(8,128)(2,1)} %all-gather.3.cloned.1.call-done, pred[128]{0:T(512)(128)(4,1)S(1)} %iota_compare_fusion.1), kind=kOutput, calls=%fused_computation.2 | convolution fusion | flops 360873984 | bytes 4227200 | tf_op jit(solution)/shard_map/dot_general | solution.py:55
  194.9 0.3 copy.10
  195.2 0.0 copy-start.4
  195.2 4.5 %convolution_bitcast_fusion = f32[32]{0:T(128)S(1)} fusion(bf16[98304,1]{0,1:T(2,128)(2,1)S(1)} %bitcast.30, bf16[32,98304]{1,0:T(8,128)(2,1)} %bitcast.28), kind=kOutput, calls=%fused_computation.6 | convolution fusion | flops 6291456 | bytes 6488192 | tf_op jit(solution)/shard_map/dot_general | solution.py:58
  199.7 0.0 copy-done.4
  199.7 0.7 select_reduce_fusion
  (2 shorter events, 0.0 us)
Async XLA Ops:
  6.5 4.3 %copy-start = (bf16[1728,512]{1,0:T(8,128)(2,1)S(1)}, bf16[1728,512]{1,0:T(8,128)(2,1)}, u32[]{:S(2)}) copy-start(bf16[1728,512]{1,0:T(8,128)(2,1)} %param.16) | copy-start | bytes 5308420
  6.5 4.3 %copy-start.1 = (bf16[1728,384]{1,0:T(8,128)(2,1)S(1)}, bf16[1728,384]{1,0:T(8,128)(2,1)}, u32[]{:S(2)}) copy-start(bf16[1728,384]{1,0:T(8,128)(2,1)} %param.13) | copy-start | bytes 3981316
  6.5 131.2 %all-gather.5.cloned.1.call-start = ((), (), s32[]{:S(2)}) async-start(), calls=%async_computation.1 | async-start | bytes 22560768 | tf_op jit(solution)/shard_map/all_gather | solution.py:51
  7.3 5.6 %copy-start.2 = (f32[256,384]{1,0:T(8,128)S(1)}, f32[256,384]{1,0:T(8,128)}, u32[]{:S(2)}) copy-start(f32[256,384]{1,0:T(8,128)} %param.14) | copy-start | bytes 1179652
  7.3 185.0 %all-gather.3.cloned.1.call-start = ((), (), s32[]{:S(2)}) async-start(), calls=%async_computation | async-start | bytes 2785280 | tf_op jit(solution)/shard_map/all_gather | solution.py:27
  101.7 90.6 %copy-start.3 = (bf16[128,5120]{1,0:T(8,128)(2,1)S(1)}, bf16[128,5120]{1,0:T(8,128)(2,1)}, u32[]{:S(2)}) copy-start(bf16[128,5120]{1,0:T(8,128)(2,1)} %param.10) | copy-start | bytes 3932164
  195.2 4.5 %copy-start.4 = (s32[1,8]{1,0:T(1,128)S(1)}, s32[1,8]{1,0:T(1,128)}, u32[]{:S(2)}) copy-start(s32[1,8]{1,0:T(1,128)} %param.17) | copy-start | bytes 100
Sparse Core Ops, SparseCore 0:
  9.0 128.7 all-gather.4
  140.0 52.2 all-gather.2
where the time goes:
time: 209 us; the launch traced here: 207 us
  waiting for transfers between devices  79.1 us (38%)
  blocking collectives  79.1 us (38%)
  matrix products  26.1 us (12%)
  between operations  14.7 us (7%)
  local copies, waits for them, and re-layouts  6.82 us (3%)
    psum x1, blocking collectives, shards(): out_total, in_total = lax.psum((out_part, in_part), 'dp')  79.1 us
    all_gather x1, waiting for transfers between devices, shards(): lax.all_gather(basis_out, 'dp', axis=0, tiled=True)  41.6 us
    all_gather x1, waiting for transfers between devices, shards(): lax.all_gather(basis_in, 'dp', axis=0, tiled=True)  36 us
    dot_general x1, matrix products, shards(): jnp.dot(columns, lax.all_gather(basis_in, 'dp', axis=0, tiled=True), pref...  12.9 us
    unnamed x12, local copies, waits for them, and re-layouts  6.82 us
    dot_general x1, matrix products, shards(): lax.dot_general(train_rot.reshape(1, rank_out * rank_in), precond, flat_c...  4.51 us
  transfers between devices with their start and end apart: 2, of which 2 were waited for; matrix products, arithmetic and copies ran while one was open for 13% of the time, Pallas kernels for 0%

commit v1 on v0

v1 whole, which is shorter than its diff:
```python
import functools

import jax
import jax.numpy as jnp
from jax import lax
from jax.experimental import pallas as pl
from jax.experimental.pallas import tpu as pltpu
from jax.sharding import PartitionSpec as P

NQ = 32
QLEN = 16
MESH = pl.DeviceIdType.MESH
CONTRACT = (((0,), (0,)), ((), ()))


def third(rows):
    return (rows + 24) // 48 * 16


def kernel(
    n,
    width,
    acts_hbm,
    grads_hbm,
    live_ref,
    basis_in,
    basis_out,
    scale_ref,
    part_ref,
    totals_ref,
    acts,
    grads,
    held_in,
    held_out,
    q_got,
    q_mine,
    q_all,
    precond,
    a_sum,
    g_sum,
    local_sem,
    q_send,
    q_recv,
    r_send,
    r_recv,
    own_send,
    own_recv,
    ring_send,
    ring_recv,
    y_send,
    y_recv,
    s_send,
    s_recv,
):
    chips = n // 2
    deep = chips // width
    half = chips // 2
    group = lax.axis_index("groups")
    me = lax.axis_index("dp")
    core = lax.rem(me, 2)
    chip = me // 2
    z, x = chip // width, lax.rem(chip, width)

    odd = lax.rem(z, 2)
    snake = z * (width - 1) + (1 - odd) * (x - 1) + odd * (width - 1 - x)
    pos = jnp.where(x == 0, chips - 1 - z, snake)

    def chip_at(place):
        place = lax.rem(place + 2 * chips, chips)
        row = place // (width - 1)
        r = lax.rem(place, width - 1)
        flip = lax.rem(row, 2)
        ahead = row * width + 1 + (1 - flip) * r + flip * (width - 2 - r)
        back = (chips - 1 - place) * width
        return jnp.where(place < (width - 1) * deep, ahead, back)

    sibling = (group, chip * 2 + 1 - core)
    across = (1 - group, me)
    ring = {d: (group, chip_at(pos + d) * 2 + core) for d in (1, -1)}

    own = (basis_in, basis_out)
    held = (held_in, held_out)
    rows = (basis_in.shape[0], basis_out.shape[0])
    cut = tuple(third(r) for r in rows)

    def span(i, piece):
        if piece == "S":
            return cut[i], rows[i] - 2 * cut[i]
        side = group if piece == "R" else 1 - group
        return pl.multiple_of(side * (rows[i] - cut[i]), 16), cut[i]

    def place(i, where, piece):
        start, size = span(i, piece)
        return held[i].at[where, pl.ds(pl.multiple_of(core * rows[i] + start, 16), size)]

    barrier = pltpu.get_barrier_semaphore()
    for k in range(1, n):
        pl.semaphore_signal(
            barrier, inc=1, device_id=(group, lax.rem(me + k, n)), device_id_type=MESH
        )
    pl.semaphore_signal(barrier, inc=1, device_id=across, device_id_type=MESH)
    local = [
        pltpu.make_async_copy(acts_hbm, acts, local_sem.at[0]),
        pltpu.make_async_copy(grads_hbm, grads, local_sem.at[1]),
        pltpu.make_async_copy(part_ref.at[me], q_got.at[me], local_sem.at[2]),
    ]
    for i in range(2):
        mine = held[i].at[chip, pl.ds(pl.multiple_of(core * rows[i], 16), rows[i])]
        local.append(pltpu.make_async_copy(own[i], mine, local_sem.at[3 + i]))
    for copy in local:
        copy.start()
    pl.semaphore_wait(barrier, n)

    sent = []

    def send(src, dst, send_sem, recv_sem, device):
        copy = pltpu.make_async_remote_copy(
            src_ref=src,
            dst_ref=dst,
            send_sem=send_sem,
            recv_sem=recv_sem,
            device_id=device,
            device_id_type=MESH,
        )
        copy.start()
        sent.append(copy)
        return copy

    def arrived(dst, recv_sem):
        pltpu.make_async_copy(dst, dst, recv_sem).wait()

    for k in range(1, n):
        to = lax.rem(me + k, n)
        send(part_ref.at[to], q_got.at[me], q_send.at[k], q_recv.at[k], (group, to))

    lane = {1: 0, -1: 1}
    letter = {"R": 0, "S": 1, "Y": 2}

    def carries(d, s, piece):
        if s < half:
            return True
        return s == half and (d == 1) == (piece == "R")

    def forward(d, s, i, piece, src):
        where = chip_at(pos - d * (s - 1))
        k = (lane[d], s - 1, i, letter[piece])
        send(src, place(i, where, piece), ring_send.at[k], ring_recv.at[k], ring[d])

    for piece in ("R", "S"):
        for i in range(2):
            start, size = span(i, piece)
            for d in (1, -1):
                if carries(d, 1, piece):
                    forward(d, 1, i, piece, own[i].at[pl.ds(start, size)])
    for i in range(2):
        mine = held[i].at[chip, pl.ds(pl.multiple_of(core * rows[i], 16), rows[i])]
        send(own[i], mine, own_send.at[i], own_recv.at[i], sibling)

    def share(d, s, i, piece):
        where = place(i, chip_at(pos - d * s), piece)
        k = (lane[d], s - 1, i, letter[piece])
        send(where, where, s_send.at[k], s_recv.at[k], sibling)

    def blocks(s):
        return ((1, s), (-1, s)) if s < half else ((1, s),)

    def relayed(s):
        for d, s in blocks(s):
            for i in range(2):
                where = place(i, chip_at(pos - d * s), "Y")
                arrived(where, y_recv.at[lane[d], s - 1, i])
                share(d, s, i, "Y")

    def multiply(where):
        tile = 3 * 128
        depth = 2 * rows[0]

        def body(t, carry):
            at = pl.multiple_of(t * tile, 128)
            a_sum[...] += jnp.dot(
                acts[:, pl.ds(pl.multiple_of(where * depth + at, 128), tile)],
                held_in[where, pl.ds(at, tile)],
                preferred_element_type=jnp.float32,
            )
            return carry

        lax.fori_loop(0, depth // tile, body, 0)
        wide = 2 * rows[1]
        g_sum[...] += jnp.dot(
            grads[:, pl.ds(pl.multiple_of(where * wide, 128), wide)],
            held_out[where],
            preferred_element_type=jnp.float32,
        )

    def shared(s):
        for d, s in blocks(s):
            where = chip_at(pos - d * s)
            for i in range(2):
                for piece in ("R", "S", "Y"):
                    dd = -1 if (s == half and piece == "S") else d
                    start, size = span(i, piece)
                    at = pl.multiple_of((1 - core) * rows[i] + start, 16)
                    arrived(
                        held[i].at[where, pl.ds(at, size)],
                        s_recv.at[lane[dd], s - 1, i, letter[piece]],
                    )
            multiply(where)

    def spread():
        for k in range(1, n):
            arrived(q_got.at[lax.rem(me - k + n, n)], q_recv.at[k])
        local[2].wait()
        q_mine[...] = jnp.sum(q_got[...].astype(jnp.float32), axis=0).astype(jnp.bfloat16)
        q_all[me] = q_mine[...]
        for k in range(1, n):
            to = lax.rem(me + k, n)
            send(q_mine, q_all.at[me], r_send.at[k], r_recv.at[k], (group, to))

    def condition():
        for k in range(1, n):
            arrived(q_all.at[lax.rem(me - k + n, n)], r_recv.at[k])
        rank_out = g_sum.shape[1]
        per = q_all.shape[1] // QLEN

        def body(device, carry):
            for u in range(per):
                tokens = q_all[device, pl.ds(u * QLEN, QLEN)]
                joint = lax.dot_general(
                    tokens[:, :rank_out],
                    tokens[:, rank_out:],
                    CONTRACT,
                    preferred_element_type=jnp.float32,
                )
                precond[device * per + u] = (joint / scale_ref[...]).astype(jnp.bfloat16)
            return carry

        lax.fori_loop(0, n, body, 0)

    a_sum[...] = jnp.zeros_like(a_sum)
    g_sum[...] = jnp.zeros_like(g_sum)
    spread()
    for s in range(1, half + 1):
        for piece in ("R", "S"):
            for d in (1, -1):
                if not carries(d, s, piece):
                    continue
                for i in range(2):
                    where = place(i, chip_at(pos - d * s), piece)
                    arrived(where, ring_recv.at[lane[d], s - 1, i, letter[piece]])
                    if carries(d, s + 1, piece):
                        forward(d, s + 1, i, piece, where)
                    if piece == "R":
                        send(
                            where,
                            where,
                            y_send.at[lane[d], s - 1, i],
                            y_recv.at[lane[d], s - 1, i],
                            across,
                        )
                    share(d, s, i, piece)
        if s > 1:
            relayed(s - 1)
        if s == 1:
            for k in (0, 1, 3, 4):
                local[k].wait()
            for i in range(2):
                at = pl.multiple_of((1 - core) * rows[i], 16)
                arrived(held[i].at[chip, pl.ds(at, rows[i])], own_recv.at[i])
            multiply(chip)
            condition()
        if s > 2:
            shared(s - 2)
    relayed(half)
    for s in range(max(1, half - 1), half + 1):
        shared(s)

    g_rot = (g_sum[...] * live_ref[...]).astype(jnp.bfloat16)
    a_rot = a_sum[...].astype(jnp.bfloat16)
    train_rot = (
        lax.dot_general(g_rot, a_rot, CONTRACT, preferred_element_type=jnp.float32)
        .astype(jnp.bfloat16)
        .astype(jnp.float32)
    )
    a_sum_rows = train_rot.shape[0]

    def score(q, carry):
        product = precond[q].astype(jnp.float32) * train_rot
        totals_ref[pl.ds(q, 1)] = jnp.sum(
            product.reshape(a_sum_rows // 8, 8, product.shape[1]), axis=0
        )[None]
        return carry

    lax.fori_loop(0, precond.shape[0], score, 0)
    for copy in sent:
        copy.wait_send()


def exchanged(n, acts, grads, live, basis_in, basis_out, scale, part):
    chips = n // 2
    width = 1
    while 8 * width * width <= chips:
        width *= 2
    half = chips // 2
    tokens = acts.shape[0]
    rank_out, rank_in = scale.shape
    share = part.shape[1:]
    dma = pltpu.SemaphoreType.DMA
    anywhere = pl.BlockSpec(memory_space=pl.ANY)
    vmem = pl.BlockSpec(memory_space=pltpu.VMEM)
    return pl.pallas_call(
        functools.partial(kernel, n, width),
        out_shape=jax.ShapeDtypeStruct((NQ, 8, rank_in), jnp.float32),
        in_specs=[anywhere, anywhere, vmem, anywhere, anywhere, vmem, vmem],
        out_specs=vmem,
        scratch_shapes=[
            pltpu.VMEM(acts.shape, jnp.bfloat16),
            pltpu.VMEM(grads.shape, jnp.bfloat16),
            pltpu.VMEM((chips, 2 * basis_in.shape[0], rank_in), jnp.bfloat16),
            pltpu.VMEM((chips, 2 * basis_out.shape[0], rank_out), jnp.bfloat16),
            pltpu.VMEM((n, *share), jnp.bfloat16),
            pltpu.VMEM(share, jnp.bfloat16),
            pltpu.VMEM((n, *share), jnp.bfloat16),
            pltpu.VMEM((NQ, rank_out, rank_in), jnp.bfloat16),
            pltpu.VMEM((tokens, rank_in), jnp.float32),
            pltpu.VMEM((tokens, rank_out), jnp.float32),
            dma((5,)),
            dma((n,)),
            dma((n,)),
            dma((n,)),
            dma((n,)),
            dma((2,)),
            dma((2,)),
            dma((2, half, 2, 2)),
            dma((2, half, 2, 2)),
            dma((2, half, 2)),
            dma((2, half, 2)),
            dma((2, half, 2, 3)),
            dma((2, half, 2, 3)),
        ],
        compiler_params=pltpu.CompilerParams(
            collective_id=0, has_side_effects=True, vmem_limit_bytes=60 * 1024 * 1024
        ),
    )(acts, grads, live, basis_in, basis_out, scale, part)


def plain(acts, grads, live, basis_in, basis_out, scale, part):
    tokens = lax.psum_scatter(part.astype(jnp.float32), "dp", scatter_dimension=0, tiled=False)
    tokens = lax.all_gather(tokens.astype(jnp.bfloat16), "dp", axis=0, tiled=True)
    rank_out = scale.shape[0]
    tokens = tokens.reshape(NQ, QLEN, -1)
    joint = jnp.einsum(
        "qui,quj->qij",
        tokens[..., :rank_out],
        tokens[..., rank_out:],
        preferred_element_type=jnp.float32,
    )
    precond = (joint / scale).astype(jnp.bfloat16)
    whole_in = lax.all_gather(basis_in, "dp", axis=0, tiled=True)
    whole_out = lax.all_gather(basis_out, "dp", axis=0, tiled=True)
    a_rot = jnp.dot(acts, whole_in, preferred_element_type=jnp.float32).astype(jnp.bfloat16)
    g_rot = jnp.dot(grads, whole_out, preferred_element_type=jnp.float32)
    g_rot = (g_rot * live).astype(jnp.bfloat16)
    train_rot = lax.dot_general(
        g_rot, a_rot, CONTRACT, preferred_element_type=jnp.float32
    ).astype(jnp.bfloat16)
    return jnp.sum(precond.astype(jnp.float32) * train_rot.astype(jnp.float32), axis=1)[:, None]


def shards(
    n,
    train_acts,
    train_grads,
    seq_lengths,
    basis_out,
    basis_in,
    eigenvalues,
    query_grads,
    query_acts,
    candidates,
):
    tok_dev = train_acts.shape[0]
    out_part = lax.dot_general(
        query_grads, basis_out, CONTRACT, preferred_element_type=jnp.float32
    ).astype(jnp.bfloat16)
    in_part = lax.dot_general(
        query_acts, basis_in, CONTRACT, preferred_element_type=jnp.float32
    ).astype(jnp.bfloat16)
    part = jnp.concatenate([out_part, in_part], axis=1)
    part = part.reshape(n, part.shape[0] // n, part.shape[1])
    live = (jnp.arange(tok_dev, dtype=jnp.int32) < seq_lengths[0])[:, None].astype(jnp.float32)
    scale = eigenvalues + 0.1 * jnp.mean(eigenvalues)
    fits = (
        n >= 8
        and n % 4 == 0
        and basis_in.shape[0] % 192 == 0
        and basis_out.shape[0] % 64 == 0
        and part.shape[1] % QLEN == 0
    )
    chosen = functools.partial(exchanged, n) if fits else plain
    totals = chosen(train_acts, train_grads, live, basis_in, basis_out, scale, part)
    totals = jnp.sum(totals, axis=(1, 2))[None, :]
    matches = candidates[:, :, None] == jnp.arange(NQ, dtype=jnp.int32)[None, None, :]
    return jnp.sum(jnp.where(matches, totals[:, None, :], jnp.zeros((), jnp.float32)), axis=2)


def solution(mesh):
    placed = (
        P(("groups", "dp"), None),
        P(("groups", "dp"), None),
        P(("groups", "dp")),
        P("dp", None),
        P("dp", None),
        P(),
        P("dp", "groups"),
        P("dp", "groups"),
        P(("groups", "dp"), None),
    )
    return jax.shard_map(
        functools.partial(shards, mesh.shape["dp"]),
        mesh=mesh,
        in_specs=placed,
        out_specs=P(("groups", "dp"), None),
        check_vma=False,
    )
```

time: 209 us -> 144 us (0.69)
  Pallas kernels: 0 us -> 133 us
  blocking collectives: 79.1 us -> 0 us
  waiting for transfers between devices: 79.1 us -> 0 us
  matrix products: 26.1 us -> 2.58 us
  between operations: 14.7 us -> 1.37 us
  local copies, waits for them, and re-layouts: 6.82 us -> 2.56 us
  other arithmetic: 1.46 us -> 4.17 us
    pallas_call x0 -> x1, Pallas kernels: none -> 133 us  [exchanged(): pl.pallas_call(functools.partial(kernel, n, width), out_shape=jax.ShapeDt...]
    psum x1 -> x0, blocking collectives: 79.1 us -> none  [shards(): out_total, in_total = lax.psum((out_part, in_part), 'dp')]
    all_gather x2 -> x0, waiting for transfers between devices: 77.7 us -> none  [the longest x1 41.6 us: shards(): lax.all_gather(basis_out, 'dp', axis=0, tiled=True)]
    dot_general x6 -> x2, matrix products: 26.1 us -> 2.58 us  [the longest x1 2.24 us: shards(): lax.dot_general(query_acts, basis_in, CONTRACT, preferred_element_type=jn...]
    unnamed x12 -> x10, local copies, waits for them, and re-layouts: 6.82 us -> 1.49 us
  transfers between devices with their start and end apart: 2 -> 0, of which waited for: 2 -> 0; matrix products, arithmetic and copies ran while one was open for 13% -> 0% of each run, Pallas kernels for 0% -> 0%
where the time goes in v1:
time: 144 us
  Pallas kernels  133 us (92%)
  other arithmetic  4.17 us (3%)
  matrix products  2.58 us (2%)
  local copies, waits for them, and re-layouts  2.56 us (2%)
    pallas_call x1, Pallas kernels, exchanged(): pl.pallas_call(functools.partial(kernel, n, width), out_shape=jax.ShapeDt...  133 us

profile of v1, /device:TPU:9, one launch (start us, length us, event | category | flops | bytes accessed | tf_op | source)
XLA Modules:
  0.0 144.1 jit_solution(18193409729696745344)
XLA Ops:
  0.0 0.0 copy-start
  0.0 0.0 copy-start.2
  0.0 0.0 copy-start.3
  0.0 1.5 %copy-done = bf16[1728,512]{1,0:T(8,128)(2,1)S(1)} copy-done((bf16[1728,512]{1,0:T(8,128)(2,1)S(1)}, bf16[1728,512]{1,0:T(8,128)(2,1)}, u32[]{:S(2)}) %copy-start) | copy-done | bytes 1769496
  1.5 2.2 %convolution_convert_fusion = bf16[512,384]{0,1:T(8,128)(2,1)S(1)} fusion(bf16[1728,512]{1,0:T(8,128)(2,1)S(1)} %copy-done, bf16[1728,384]{1,0:T(8,128)(2,1)} %basis_in.1), kind=kOutput, calls=%fused_computation | convolution fusion | flops 679673856 | bytes 3489792 | tf_op jit(solution)/shard_map/dot_general | solution.py:385
  3.7 0.0 copy-done.2
  3.7 0.0 copy-done.3
  3.7 0.3 convolution_convert_fusion.1
  4.1 0.0 copy-start.1
  4.2 1.1 copy.11
  5.2 0.0 copy-done.1
  5.2 0.7 reduce_sum.29
  6.6 0.8 broadcast_add_fusion.scale_ref
  8.0 0.6 fusion.live_ref
  8.7 0.0 copy-start.4
  8.7 133.4 %shard_map.94 = f32[32,8,384]{2,1,0:T(8,128)} custom-call(bf16[128,27648]{1,0:T(8,128)(2,1)} %acts_hbm.1, bf16[128,5120]{1,0:T(8,128)(2,1)} %grads_hbm.1, f32[128,1]{1,0:T(8,128)} %fusion.live_ref, bf16[1728,384]{1,0:T(8,128)(2,1)} %basis_in.1, bf16[320,256]{1,0:T(8,128)(2,1)} %basis_out.1, f32[256,384]{1,0:T(8,128)} %broadcast_add_fusion.scale_ref, ...), custom_call_target="tpu_custom_call" | custom-call | tf_op jit(solution)/shard_map/pallas_call | solution.py:310
  142.0 1.3 reduce_sum.30
  143.4 0.0 copy-done.4
  143.4 0.7 select_reduce_fusion
  (1 shorter events, 0.0 us)
Async XLA Ops:
  0.0 1.5 %copy-start = (bf16[1728,512]{1,0:T(8,128)(2,1)S(1)}, bf16[1728,512]{1,0:T(8,128)(2,1)}, u32[]{:S(2)}) copy-start(bf16[1728,512]{1,0:T(8,128)(2,1)} %param.16) | copy-start | bytes 5308420
  0.0 3.7 %copy-start.2 = (bf16[320,256]{1,0:T(8,128)(2,1)S(1)}, bf16[320,256]{1,0:T(8,128)(2,1)}, u32[]{:S(2)}) copy-start(bf16[320,256]{1,0:T(8,128)(2,1)} %basis_out.1) | copy-start | bytes 491524
  0.0 3.7 %copy-start.3 = (bf16[320,512]{1,0:T(8,128)(2,1)S(1)}, bf16[320,512]{1,0:T(8,128)(2,1)}, u32[]{:S(2)}) copy-start(bf16[320,512]{1,0:T(8,128)(2,1)} %param.15) | copy-start | bytes 983044
  4.1 1.1 copy-start.1
  8.7 134.7 %copy-start.4 = (s32[1,8]{1,0:T(1,128)S(1)}, s32[1,8]{1,0:T(1,128)}, u32[]{:S(2)}) copy-start(s32[1,8]{1,0:T(1,128)} %param.17) | copy-start | bytes 100

commit v2 on v1

--- a/solution.py
+++ b/solution.py
@@ -22,27 +22,38 @@
     width,
     acts_hbm,
     grads_hbm,
-    live_ref,
+    lengths_ref,
     basis_in,
     basis_out,
-    scale_ref,
-    part_ref,
+    eigen_ref,
+    q_grads_hbm,
+    q_acts_hbm,
     totals_ref,
     acts,
     grads,
+    q_grads,
+    q_acts,
     held_in,
     held_out,
+    part,
+    q_half,
+    q_pre,
     q_got,
     q_mine,
     q_all,
+    inverse,
     precond,
     a_sum,
     g_sum,
     local_sem,
+    half_send,
+    half_recv,
     q_send,
     q_recv,
     r_send,
     r_recv,
+    pass_send,
+    pass_recv,
     own_send,
     own_recv,
     ring_send,
@@ -94,22 +105,20 @@
         return held[i].at[where, pl.ds(pl.multiple_of(core * rows[i] + start, 16), size)]
 
     barrier = pltpu.get_barrier_semaphore()
-    for k in range(1, n):
-        pl.semaphore_signal(
-            barrier, inc=1, device_id=(group, lax.rem(me + k, n)), device_id_type=MESH
-        )
-    pl.semaphore_signal(barrier, inc=1, device_id=across, device_id_type=MESH)
-    local = [
-        pltpu.make_async_copy(acts_hbm, acts, local_sem.at[0]),
-        pltpu.make_async_copy(grads_hbm, grads, local_sem.at[1]),
-        pltpu.make_async_copy(part_ref.at[me], q_got.at[me], local_sem.at[2]),
-    ]
+    peers = [(k, lax.rem(chip + k, chips)) for k in range(1, chips)]
+    for device in [(group, to * 2 + core) for _, to in peers] + [sibling, across]:
+        pl.semaphore_signal(barrier, inc=1, device_id=device, device_id_type=MESH)
+    local = []
     for i in range(2):
         mine = held[i].at[chip, pl.ds(pl.multiple_of(core * rows[i], 16), rows[i])]
-        local.append(pltpu.make_async_copy(own[i], mine, local_sem.at[3 + i]))
+        local.append(pltpu.make_async_copy(own[i], mine, local_sem.at[i]))
+    local.append(pltpu.make_async_copy(q_grads_hbm, q_grads, local_sem.at[2]))
+    local.append(pltpu.make_async_copy(q_acts_hbm, q_acts, local_sem.at[3]))
+    local.append(pltpu.make_async_copy(acts_hbm, acts, local_sem.at[4]))
+    local.append(pltpu.make_async_copy(grads_hbm, grads, local_sem.at[5]))
     for copy in local:
         copy.start()
-    pl.semaphore_wait(barrier, n)
+    pl.semaphore_wait(barrier, chips + 1)
 
     sent = []
 
@@ -128,10 +137,6 @@
 
     def arrived(dst, recv_sem):
         pltpu.make_async_copy(dst, dst, recv_sem).wait()
-
-    for k in range(1, n):
-        to = lax.rem(me + k, n)
-        send(part_ref.at[to], q_got.at[me], q_send.at[k], q_recv.at[k], (group, to))
 
     lane = {1: 0, -1: 1}
     letter = {"R": 0, "S": 1, "Y": 2}
@@ -206,19 +211,63 @@
                     )
             multiply(where)
 
+    def queries():
+        for copy in local[:4]:
+            copy.wait()
+        share_rows = part.shape[1]
+        rank_out = g_sum.shape[1]
+        tile = 128
+        mine = [pl.ds(pl.multiple_of(core * r, 16), r) for r in rows]
+
+        def body(t, carry):
+            columns = pl.ds(pl.multiple_of(t * tile, tile), tile)
+            first = lax.dot_general(
+                q_grads[:, columns],
+                held_out[chip, mine[1]],
+                CONTRACT,
+                preferred_element_type=jnp.float32,
+            ).astype(jnp.bfloat16)
+            second = lax.dot_general(
+                q_acts[:, columns],
+                held_in[chip, mine[0]],
+                CONTRACT,
+                preferred_element_type=jnp.float32,
+            ).astype(jnp.bfloat16)
+            for u in range(tile // share_rows):
+                at = slice(u * share_rows, (u + 1) * share_rows)
+                part[t * (tile // share_rows) + u, :, :rank_out] = first[at]
+                part[t * (tile // share_rows) + u, :, rank_out:] = second[at]
+            return carry
+
+        lax.fori_loop(0, q_acts.shape[1] // tile, body, 0)
+        theirs = part.at[pl.ds((1 - core) * chips, chips)]
+        send(theirs, q_half, half_send.at[0], half_recv.at[0], sibling)
+
+    def scatter():
+        arrived(q_half, half_recv.at[0])
+        mine = part[pl.ds(core * chips, chips)].astype(jnp.float32)
+        q_pre[...] = (mine + q_half[...].astype(jnp.float32)).astype(jnp.bfloat16)
+        q_got[chip] = q_pre[chip]
+        for k, to in peers:
+            send(q_pre.at[to], q_got.at[chip], q_send.at[k], q_recv.at[k], (group, to * 2 + core))
+
     def spread():
-        for k in range(1, n):
-            arrived(q_got.at[lax.rem(me - k + n, n)], q_recv.at[k])
-        local[2].wait()
+        for k in range(1, chips):
+            arrived(q_got.at[lax.rem(chip - k + chips, chips)], q_recv.at[k])
         q_mine[...] = jnp.sum(q_got[...].astype(jnp.float32), axis=0).astype(jnp.bfloat16)
-        q_all[me] = q_mine[...]
-        for k in range(1, n):
-            to = lax.rem(me + k, n)
-            send(q_mine, q_all.at[me], r_send.at[k], r_recv.at[k], (group, to))
+        q_all[core * chips + chip] = q_mine[...]
+        slot = q_all.at[core * chips + chip]
+        for k, to in peers:
+            send(q_mine, slot, r_send.at[k], r_recv.at[k], (group, to * 2 + core))
+
+    def collect():
+        for k in range(1, chips):
+            arrived(q_all.at[core * chips + lax.rem(chip - k + chips, chips)], r_recv.at[k])
+        ours = q_all.at[pl.ds(core * chips, chips)]
+        send(ours, ours, pass_send.at[0], pass_recv.at[0], sibling)
 
     def condition():
-        for k in range(1, n):
-            arrived(q_all.at[lax.rem(me - k + n, n)], r_recv.at[k])
+        arrived(q_all.at[pl.ds((1 - core) * chips, chips)], pass_recv.at[0])
         rank_out = g_sum.shape[1]
         per = q_all.shape[1] // QLEN
 
@@ -231,14 +280,17 @@
                     CONTRACT,
                     preferred_element_type=jnp.float32,
                 )
-                precond[device * per + u] = (joint / scale_ref[...]).astype(jnp.bfloat16)
+                precond[device * per + u] = (joint * inverse[...]).astype(jnp.bfloat16)
             return carry
 
         lax.fori_loop(0, n, body, 0)
 
     a_sum[...] = jnp.zeros_like(a_sum)
     g_sum[...] = jnp.zeros_like(g_sum)
-    spread()
+    eigen = eigen_ref[...]
+    inverse[...] = 1.0 / (eigen + 0.1 * jnp.mean(eigen))
+    queries()
+    scatter()
     for s in range(1, half + 1):
         for piece in ("R", "S"):
             for d in (1, -1):
@@ -261,20 +313,25 @@
         if s > 1:
             relayed(s - 1)
         if s == 1:
-            for k in (0, 1, 3, 4):
-                local[k].wait()
+            spread()
+            for copy in local[4:]:
+                copy.wait()
             for i in range(2):
                 at = pl.multiple_of((1 - core) * rows[i], 16)
                 arrived(held[i].at[chip, pl.ds(at, rows[i])], own_recv.at[i])
             multiply(chip)
+        if s == 2:
+            collect()
+        if s == 3:
             condition()
         if s > 2:
             shared(s - 2)
+    shared(half - 1)
     relayed(half)
-    for s in range(max(1, half - 1), half + 1):
-        shared(s)
-
-    g_rot = (g_sum[...] * live_ref[...]).astype(jnp.bfloat16)
+    shared(half)
+
+    living = lax.broadcasted_iota(jnp.int32, g_sum.shape, 0) < lengths_ref[0]
+    g_rot = jnp.where(living, g_sum[...], 0.0).astype(jnp.bfloat16)
     a_rot = a_sum[...].astype(jnp.bfloat16)
     train_rot = (
         lax.dot_general(g_rot, a_rot, CONTRACT, preferred_element_type=jnp.float32)
@@ -285,9 +342,8 @@
 
     def score(q, carry):
         product = precond[q].astype(jnp.float32) * train_rot
-        totals_ref[pl.ds(q, 1)] = jnp.sum(
-            product.reshape(a_sum_rows // 8, 8, product.shape[1]), axis=0
-        )[None]
+        folded = jnp.sum(product.reshape(a_sum_rows // 8, 8, product.shape[1]), axis=0)
+        totals_ref[pl.ds(q, 1)] = folded[None]
         return carry
 
     lax.fori_loop(0, precond.shape[0], score, 0)
@@ -295,39 +351,58 @@
         copy.wait_send()
 
 
-def exchanged(n, acts, grads, live, basis_in, basis_out, scale, part):
+def exchanged(n, acts, grads, lengths, basis_in, basis_out, eigen, q_grads, q_acts):
     chips = n // 2
     width = 1
     while 8 * width * width <= chips:
         width *= 2
     half = chips // 2
     tokens = acts.shape[0]
-    rank_out, rank_in = scale.shape
-    share = part.shape[1:]
+    rank_out, rank_in = eigen.shape
+    share = (q_acts.shape[1] // n, rank_out + rank_in)
     dma = pltpu.SemaphoreType.DMA
     anywhere = pl.BlockSpec(memory_space=pl.ANY)
     vmem = pl.BlockSpec(memory_space=pltpu.VMEM)
     return pl.pallas_call(
         functools.partial(kernel, n, width),
         out_shape=jax.ShapeDtypeStruct((NQ, 8, rank_in), jnp.float32),
-        in_specs=[anywhere, anywhere, vmem, anywhere, anywhere, vmem, vmem],
+        in_specs=[
+            anywhere,
+            anywhere,
+            pl.BlockSpec(memory_space=pltpu.SMEM),
+            anywhere,
+            anywhere,
+            vmem,
+            anywhere,
+            anywhere,
+        ],
         out_specs=vmem,
         scratch_shapes=[
             pltpu.VMEM(acts.shape, jnp.bfloat16),
             pltpu.VMEM(grads.shape, jnp.bfloat16),
+            pltpu.VMEM(q_grads.shape, jnp.bfloat16),
+            pltpu.VMEM(q_acts.shape, jnp.bfloat16),
             pltpu.VMEM((chips, 2 * basis_in.shape[0], rank_in), jnp.bfloat16),
             pltpu.VMEM((chips, 2 * basis_out.shape[0], rank_out), jnp.bfloat16),
             pltpu.VMEM((n, *share), jnp.bfloat16),
+            pltpu.VMEM((chips, *share), jnp.bfloat16),
+            pltpu.VMEM((chips, *share), jnp.bfloat16),
+            pltpu.VMEM((chips, *share), jnp.bfloat16),
             pltpu.VMEM(share, jnp.bfloat16),
             pltpu.VMEM((n, *share), jnp.bfloat16),
+            pltpu.VMEM((rank_out, rank_in), jnp.float32),
             pltpu.VMEM((NQ, rank_out, rank_in), jnp.bfloat16),
             pltpu.VMEM((tokens, rank_in), jnp.float32),
             pltpu.VMEM((tokens, rank_out), jnp.float32),
-            dma((5,)),
-            dma((n,)),
-            dma((n,)),
-            dma((n,)),
-            dma((n,)),
+            dma((6,)),
+            dma((1,)),
+            dma((1,)),
+            dma((chips,)),
+            dma((chips,)),
+            dma((chips,)),
+            dma((chips,)),
+            dma((1,)),
+            dma((1,)),
             dma((2,)),
             dma((2,)),
             dma((2, half, 2, 2)),
@@ -340,11 +415,20 @@
         compiler_params=pltpu.CompilerParams(
             collective_id=0, has_side_effects=True, vmem_limit_bytes=60 * 1024 * 1024
         ),
-    )(acts, grads, live, basis_in, basis_out, scale, part)
-
-
-def plain(acts, grads, live, basis_in, basis_out, scale, part):
-    tokens = lax.psum_scatter(part.astype(jnp.float32), "dp", scatter_dimension=0, tiled=False)
+    )(acts, grads, lengths, basis_in, basis_out, eigen, q_grads, q_acts)
+
+
+def plain(acts, grads, lengths, basis_in, basis_out, eigen, q_grads, q_acts):
+    live = (jnp.arange(acts.shape[0], dtype=jnp.int32) < lengths[0])[:, None]
+    scale = eigen + 0.1 * jnp.mean(eigen)
+    part = jnp.concatenate(
+        [
+            lax.dot_general(q_grads, basis_out, CONTRACT, preferred_element_type=jnp.float32),
+            lax.dot_general(q_acts, basis_in, CONTRACT, preferred_element_type=jnp.float32),
+        ],
+        axis=1,
+    )
+    tokens = lax.psum_scatter(part, "dp", scatter_dimension=0, tiled=True)
     tokens = lax.all_gather(tokens.astype(jnp.bfloat16), "dp", axis=0, tiled=True)
     rank_out = scale.shape[0]
     tokens = tokens.reshape(NQ, QLEN, -1)
@@ -359,7 +443,7 @@
     whole_out = lax.all_gather(basis_out, "dp", axis=0, tiled=True)
     a_rot = jnp.dot(acts, whole_in, preferred_element_type=jnp.float32).astype(jnp.bfloat16)
     g_rot = jnp.dot(grads, whole_out, preferred_element_type=jnp.float32)
-    g_rot = (g_rot * live).astype(jnp.bfloat16)
+    g_rot = jnp.where(live, g_rot, 0.0).astype(jnp.bfloat16)
     train_rot = lax.dot_general(
         g_rot, a_rot, CONTRACT, preferred_element_type=jnp.float32
     ).astype(jnp.bfloat16)
@@ -378,26 +462,26 @@
     query_acts,
     candidates,
 ):
-    tok_dev = train_acts.shape[0]
-    out_part = lax.dot_general(
-        query_grads, basis_out, CONTRACT, preferred_element_type=jnp.float32
-    ).astype(jnp.bfloat16)
-    in_part = lax.dot_general(
-        query_acts, basis_in, CONTRACT, preferred_element_type=jnp.float32
-    ).astype(jnp.bfloat16)
-    part = jnp.concatenate([out_part, in_part], axis=1)
-    part = part.reshape(n, part.shape[0] // n, part.shape[1])
-    live = (jnp.arange(tok_dev, dtype=jnp.int32) < seq_lengths[0])[:, None].astype(jnp.float32)
-    scale = eigenvalues + 0.1 * jnp.mean(eigenvalues)
+    tokens = query_acts.shape[1]
     fits = (
-        n >= 8
-        and n % 4 == 0
+        n >= 16
+        and n & (n - 1) == 0
         and basis_in.shape[0] % 192 == 0
         and basis_out.shape[0] % 64 == 0
-        and part.shape[1] % QLEN == 0
+        and tokens % 128 == 0
+        and tokens // n in (QLEN, 2 * QLEN, 4 * QLEN, 8 * QLEN)
     )
     chosen = functools.partial(exchanged, n) if fits else plain
-    totals = chosen(train_acts, train_grads, live, basis_in, basis_out, scale, part)
+    totals = chosen(
+        train_acts,
+        train_grads,
+        seq_lengths,
+        basis_in,
+        basis_out,
+        eigenvalues,
+        query_grads,
+        query_acts,
+    )
     totals = jnp.sum(totals, axis=(1, 2))[None, :]
     matches = candidates[:, :, None] == jnp.arange(NQ, dtype=jnp.int32)[None, None, :]
     return jnp.sum(jnp.where(matches, totals[:, None, :], jnp.zeros((), jnp.float32)), axis=2)

time: 144 us -> 117 us (0.81)
  Pallas kernels: 133 us -> 114 us
  matrix products: 2.58 us -> 0 us
  local copies, waits for them, and re-layouts: 2.56 us -> 0.01 us
  other arithmetic: 4.17 us -> 2.01 us
    pallas_call x1, Pallas kernels: 133 us -> 114 us  [exchanged(): pl.pallas_call(functools.partial(kernel, n, width), out_shape=jax.ShapeDt...]
    dot_general x2 -> x0, matrix products: 2.58 us -> none  [the longest x1 2.24 us: shards(): lax.dot_general(query_acts, basis_in, CONTRACT, preferred_element_type=jn...]
    unnamed x10 -> x2, local copies, waits for them, and re-layouts: 1.49 us -> 0.01 us
where the time goes in v2:
time: 117 us
  Pallas kernels  114 us (97%)
  other arithmetic  2.01 us (2%)
    pallas_call x1, Pallas kernels, exchanged(): pl.pallas_call(functools.partial(kernel, n, width), out_shape=jax.ShapeDt...  114 us

profile of v2, /device:TPU:9, one launch (start us, length us, event | category | flops | bytes accessed | tf_op | source)
XLA Modules:
  0.0 116.8 jit_solution(593331717554433263)
XLA Ops:
  0.7 0.0 copy-start
  0.7 114.2 %shard_map.94 = f32[32,8,384]{2,1,0:T(8,128)} custom-call(bf16[128,27648]{1,0:T(8,128)(2,1)} %acts_hbm.1, bf16[128,5120]{1,0:T(8,128)(2,1)} %grads_hbm.1, s32[1]{0:T(128)S(6)} %copy.10.lengths_ref, bf16[1728,384]{1,0:T(8,128)(2,1)} %basis_in.1, bf16[320,256]{1,0:T(8,128)(2,1)} %basis_out.1, f32[256,384]{1,0:T(8,128)} %eigen_ref.1, ...), custom_call_target="tpu_custom_call" | custom-call | tf_op jit(solution)/shard_map/pallas_call | solution.py:366
  114.8 1.3 %reduce_sum.20 = f32[32]{0:T(128)S(1)} reduce(f32[32,8,384]{2,1,0:T(8,128)} %shard_map.94, f32[]{:T(128)} %constant.0.clone.1), dimensions={1,2}, to_apply=%region_0.0 | reduce | flops 98272 | bytes 393348 | tf_op jit(solution)/shard_map/reduce_sum | solution.py:485
  116.1 0.0 copy-done
  116.1 0.7 select_reduce_fusion
Async XLA Ops:
  0.7 115.5 %copy-start = (s32[1,8]{1,0:T(1,128)S(1)}, s32[1,8]{1,0:T(1,128)}, u32[]{:S(2)}) copy-start(s32[1,8]{1,0:T(1,128)} %param.17) | copy-start | bytes 100

commit v3 on v2

--- a/solution.py
+++ b/solution.py
@@ -177,7 +177,7 @@
                 share(d, s, i, "Y")
 
     def multiply(where):
-        tile = 3 * 128
+        tile = 9 * 128 if rows[0] % 576 == 0 else 3 * 128
         depth = 2 * rows[0]
 
         def body(t, carry):
@@ -343,10 +343,12 @@
     def score(q, carry):
         product = precond[q].astype(jnp.float32) * train_rot
         folded = jnp.sum(product.reshape(a_sum_rows // 8, 8, product.shape[1]), axis=0)
+        lanes = totals_ref.shape[2]
+        folded = sum(folded[:, at : at + lanes] for at in range(0, folded.shape[1], lanes))
         totals_ref[pl.ds(q, 1)] = folded[None]
         return carry
 
-    lax.fori_loop(0, precond.shape[0], score, 0)
+    lax.fori_loop(0, precond.shape[0], score, 0, unroll=2)
     for copy in sent:
         copy.wait_send()
 
@@ -365,7 +367,7 @@
     vmem = pl.BlockSpec(memory_space=pltpu.VMEM)
     return pl.pallas_call(
         functools.partial(kernel, n, width),
-        out_shape=jax.ShapeDtypeStruct((NQ, 8, rank_in), jnp.float32),
+        out_shape=jax.ShapeDtypeStruct((NQ, 8, 128), jnp.float32),
         in_specs=[
             anywhere,
             anywhere,
@@ -469,6 +471,7 @@
         and basis_in.shape[0] % 192 == 0
         and basis_out.shape[0] % 64 == 0
         and tokens % 128 == 0
+        and eigenvalues.shape[1] % 128 == 0
         and tokens // n in (QLEN, 2 * QLEN, 4 * QLEN, 8 * QLEN)
     )
     chosen = functools.partial(exchanged, n) if fits else plain

time: 117 us -> 116 us (level)
    pallas_call x1, Pallas kernels: 114 us -> 113 us  [exchanged(): pl.pallas_call(functools.partial(kernel, n, width), out_shape=jax.ShapeDt...]
where the time goes in v3:
time: 116 us; the launch traced here: 115 us
  Pallas kernels  113 us (97%)
  other arithmetic  1.92 us (2%)
    pallas_call x1, Pallas kernels, exchanged(): pl.pallas_call(functools.partial(kernel, n, width), out_shape=jax.ShapeDt...  113 us

profile of v3, /device:TPU:9, one launch (start us, length us, event | category | flops | bytes accessed | tf_op | source)
XLA Modules:
  0.0 115.4 jit_solution(8464807418239102861)
XLA Ops:
  0.7 0.0 copy-start
  0.7 112.8 %shard_map.94 = f32[32,8,128]{2,1,0:T(8,128)} custom-call(bf16[128,27648]{1,0:T(8,128)(2,1)} %acts_hbm.1, bf16[128,5120]{1,0:T(8,128)(2,1)} %grads_hbm.1, s32[1]{0:T(128)S(6)} %copy.10.lengths_ref, bf16[1728,384]{1,0:T(8,128)(2,1)} %basis_in.1, bf16[320,256]{1,0:T(8,128)(2,1)} %basis_out.1, f32[256,384]{1,0:T(8,128)} %eigen_ref.1, ...), custom_call_target="tpu_custom_call" | custom-call | tf_op jit(solution)/shard_map/pallas_call | solution.py:368
  113.5 1.2 %reduce_sum.20 = f32[32]{0:T(128)S(1)} reduce(f32[32,8,128]{2,1,0:T(8,128)} %shard_map.94, f32[]{:T(128)} %constant.0.clone.1), dimensions={1,2}, to_apply=%region_0.0 | reduce | flops 32736 | bytes 131204 | tf_op jit(solution)/shard_map/reduce_sum | solution.py:488
  114.7 0.0 copy-done
  114.7 0.7 select_reduce_fusion
Async XLA Ops:
  0.7 114.0 %copy-start = (s32[1,8]{1,0:T(1,128)S(1)}, s32[1,8]{1,0:T(1,128)}, u32[]{:S(2)}) copy-start(s32[1,8]{1,0:T(1,128)} %param.17) | copy-start | bytes 100
